TPU v7x, 512 devices: a whole 4x8x8 slice. The times are simulated.
512 devices in a mesh: head: 2 (over core), ctx: 256 (over y, x, z).
Axes of the slice: x: 4, y: 8, z: 8, core: 2. Of those that a mesh axis runs over, the one named last changes fastest.
Arguments:
- queries: bfloat16 [32768, 4096], P('ctx', 'head'), may hold values from -4.5 to 4.5
- key_rows: bfloat16 [32768, 512], P('ctx'), may hold values from -4.5 to 4.5
- value_rows: bfloat16 [32768, 512], P('ctx'), may hold values from -4.5 to 4.5
- out_grad: bfloat16 [32768, 4096], P('ctx', 'head'), may hold values from -6 to 6
- partner_keep: int32 [256, 3], P('ctx'), may hold values 0 or 1
Outputs:
- attended: bfloat16 [32768, 4096], P('ctx', 'head')
- query_grad: bfloat16 [32768, 4096], P('ctx', 'head')
- key_grad: bfloat16 [32768, 512], P('ctx')
- value_grad: bfloat16 [32768, 512], P('ctx')
All inputs are finite; a program needn't handle non-finite values. No bound on the sum of `partner_keep` on one device may be relied on, other than what follows from the above.
Results may differ from a plain program's by a relative error of at most 0.0093.
The roundings to bfloat16 on the way count: a program that leaves them out, or rounds other values in their place, can miss the bound.
Values may be sent and summed in bfloat16 or wider, within the bound.
No kernel may reach another device: no remote copies, remote signals or barrier semaphores. Data moves between devices by JAX's collectives and lax.ppermute only.
A program may use at most 64 MiB of HBM per device.

v0:
```python
import jax
import jax.numpy as jnp
from jax import lax
from jax.sharding import PartitionSpec as P

HD = 128
POOL = 32
LEVELS = 3


def shifted(value, axis, steps):
    count = lax.axis_size(axis)
    leading, last = (max(0, -steps), min(count, count - steps))
    return lax.ppermute(value, axis, [(source, source + steps) for source in range(leading, last)])


def head_slice(matrix, head_index, col_width):
    return matrix[:, head_index * col_width : (head_index + 1) * col_width]


def masked_scores(query_rows, key_block, live_mask, score_scale):
    raw_scores = jnp.einsum("rd,kd->rk", query_rows, key_block, preferred_element_type=jnp.float32)
    return jnp.where(live_mask, raw_scores * score_scale, -jnp.inf)


def local_live(first_row, row_total, group_size, tok_dev, live_cols):
    positions = (first_row + lax.iota(jnp.int32, row_total)) // group_size
    columns = lax.iota(jnp.int32, live_cols.shape[0])
    return jnp.where(
        columns[None, :] < tok_dev, columns[None, :] <= positions[:, None], live_cols[None, :]
    )


def per_head_blocks(section_fn, head_total, arrays):
    results = []
    for head_index in range(head_total):
        sliced = tuple((array_item[head_index] for array_item in arrays))
        numbers = jnp.arange(sliced[0].shape[0], dtype=jnp.int32)

        def inner_step(packed, head_index=head_index):
            return section_fn(head_index, packed[0], *packed[1:])

        results.append(lax.map(inner_step, (numbers,) + sliced))
    return jax.tree.map(lambda *pieces_list: jnp.stack(pieces_list), *results)


def local(queries, key_rows, value_rows, out_grad, partner_keep):
    ctx_count = lax.axis_size("ctx")
    block_id = lax.axis_index("ctx")
    kv_width = key_rows.shape[1] // lax.axis_size("head")
    head_total = kv_width // HD
    tok_dev = queries.shape[0]
    group_size = queries.shape[1] // kv_width
    score_scale = HD ** (-0.5)
    row_count = tok_dev * group_size
    row_block = min(row_count, 512)
    block_count = row_count // row_block
    land_dev = tok_dev // POOL
    col_start = lax.axis_index("head") * kv_width
    own_keys = lax.dynamic_slice_in_dim(key_rows, col_start, kv_width, 1)
    own_values = lax.dynamic_slice_in_dim(value_rows, col_start, kv_width, 1)
    land_keys = (
        own_keys.astype(jnp.float32)
        .reshape(land_dev, POOL, kv_width)
        .mean(axis=1)
        .astype(jnp.bfloat16)
    )
    land_values = (
        own_values.astype(jnp.float32)
        .reshape(land_dev, POOL, kv_width)
        .mean(axis=1)
        .astype(jnp.bfloat16)
    )
    key_parts = [own_keys]
    value_parts = [own_values]
    live_parts = [jnp.ones((tok_dev,), jnp.bool_)]
    distances = []
    for level_index in range(LEVELS):
        distance = ctx_count // 2 ** (level_index + 1)
        distances.append(distance)
        arrived = shifted((own_keys, own_values), "ctx", distance)
        key_parts.append(arrived[0])
        value_parts.append(arrived[1])
        earlier = block_id // distance % 2 == 1
        wanted = jnp.logical_and(earlier, partner_keep[0, level_index] == 1)
        live_parts.append(jnp.broadcast_to(wanted, (tok_dev,)))
    local_keys = jnp.concatenate(key_parts, axis=0)
    local_values = jnp.concatenate(value_parts, axis=0)
    live_cols = jnp.concatenate(live_parts)

    def to_grid(matrix):
        return jnp.stack(
            [
                head_slice(matrix, head_index, group_size * HD).reshape(block_count, row_block, HD)
                for head_index in range(head_total)
            ]
        )

    def from_grid(grid_rows):
        return jnp.concatenate(
            [
                grid_rows[head_index].reshape(tok_dev, group_size * HD)
                for head_index in range(head_total)
            ],
            axis=1,
        )

    query_grid = to_grid(queries)
    dout_grid = to_grid(out_grad)

    def local_mask(number):
        return local_live(number * row_block, row_block, group_size, tok_dev, live_cols)

    def land_mask(land_total):
        return (lax.iota(jnp.int32, land_total) // land_dev < block_id)[None, :]

    def land_pass(section_fn, initial):
        result = section_fn(
            initial,
            (
                lax.all_gather(land_keys, "ctx", axis=0, tiled=True),
                lax.all_gather(land_values, "ctx", axis=0, tiled=True),
            ),
            jnp.int32(0),
        )
        return result

    def local_stats(head_index, number, query_blk):
        scores = masked_scores(
            query_blk, head_slice(local_keys, head_index, HD), local_mask(number), score_scale
        )
        peak_rows = jnp.max(scores, axis=1)
        return (peak_rows, jnp.sum(jnp.exp(scores - peak_rows[:, None]), axis=1))

    peaks, totals = per_head_blocks(local_stats, head_total, (query_grid,))

    def land_stats(carried, land_piece, first_land):
        live_mask = land_mask(land_piece[0].shape[0])

        def update(head_index, number, query_blk, peak_blk, total_blk):
            scores = masked_scores(
                query_blk, head_slice(land_piece[0], head_index, HD), live_mask, score_scale
            )
            peak_rows = jnp.maximum(peak_blk, jnp.max(scores, axis=1))
            return (
                peak_rows,
                total_blk * jnp.exp(peak_blk - peak_rows)
                + jnp.sum(jnp.exp(scores - peak_rows[:, None]), axis=1),
            )

        return per_head_blocks(update, head_total, (query_grid, carried[0], carried[1]))

    peaks, totals = land_pass(land_stats, (peaks, totals))
    log_sums = peaks + jnp.log(totals)

    def local_output(head_index, number, query_blk, lse_blk):
        scores = masked_scores(
            query_blk, head_slice(local_keys, head_index, HD), local_mask(number), score_scale
        )
        soft_half = jnp.exp(scores - lse_blk[:, None]).astype(jnp.bfloat16)
        return (
            jnp.dot(
                soft_half,
                head_slice(local_values, head_index, HD),
                preferred_element_type=jnp.float32,
            ),
        )

    (output_sums,) = per_head_blocks(local_output, head_total, (query_grid, log_sums))

    def land_output(carried, land_piece, first_land):
        live_mask = land_mask(land_piece[0].shape[0])

        def update(head_index, number, query_blk, lse_blk, sum_blk):
            scores = masked_scores(
                query_blk, head_slice(land_piece[0], head_index, HD), live_mask, score_scale
            )
            soft_half = jnp.exp(scores - lse_blk[:, None]).astype(jnp.bfloat16)
            return (
                sum_blk
                + jnp.dot(
                    soft_half,
                    head_slice(land_piece[1], head_index, HD),
                    preferred_element_type=jnp.float32,
                ),
            )

        return per_head_blocks(update, head_total, (query_grid, log_sums, carried[0]))

    (output_sums,) = land_pass(land_output, (output_sums,))
    out_grid = output_sums.astype(jnp.bfloat16)

    def local_backward(head_index, number, query_blk, dout_blk, lse_blk, out_blk):
        key_slice = head_slice(local_keys, head_index, HD)
        value_slice = head_slice(local_values, head_index, HD)
        scores = masked_scores(query_blk, key_slice, local_mask(number), score_scale)
        soft_full = jnp.exp(scores - lse_blk[:, None])
        soft_half = soft_full.astype(jnp.bfloat16)
        delta_rows = jnp.sum(dout_blk.astype(jnp.float32) * out_blk.astype(jnp.float32), axis=1)
        dsoft = jnp.einsum("rd,kd->rk", dout_blk, value_slice, preferred_element_type=jnp.float32)
        dscores = (soft_full * (dsoft - delta_rows[:, None])).astype(jnp.bfloat16)
        query_part = score_scale * jnp.dot(dscores, key_slice, preferred_element_type=jnp.float32)
        key_part = score_scale * jnp.einsum(
            "rk,rd->kd", dscores, query_blk, preferred_element_type=jnp.float32
        )
        value_part = jnp.einsum(
            "rk,rd->kd", soft_half, dout_blk, preferred_element_type=jnp.float32
        )
        return (query_part, key_part, value_part, delta_rows)

    query_sums, key_terms, value_terms, deltas = per_head_blocks(
        local_backward, head_total, (query_grid, dout_grid, log_sums, out_grid)
    )

    def land_backward(carried, land_piece, first_land):
        live_mask = land_mask(land_piece[0].shape[0])

        def update(head_index, number, query_blk, dout_blk, lse_blk, delta_blk, sum_blk):
            key_slice = head_slice(land_piece[0], head_index, HD)
            scores = masked_scores(query_blk, key_slice, live_mask, score_scale)
            soft_full = jnp.exp(scores - lse_blk[:, None])
            dsoft = jnp.einsum(
                "rd,kd->rk",
                dout_blk,
                head_slice(land_piece[1], head_index, HD),
                preferred_element_type=jnp.float32,
            )
            dscores = (soft_full * (dsoft - delta_blk[:, None])).astype(jnp.bfloat16)
            return (
                sum_blk
                + score_scale * jnp.dot(dscores, key_slice, preferred_element_type=jnp.float32),
            )

        return per_head_blocks(
            update, head_total, (query_grid, dout_grid, log_sums, deltas, carried[0])
        )

    (query_sums,) = land_pass(land_backward, (query_sums,))
    key_local = jnp.sum(key_terms, axis=1).transpose(1, 0, 2).reshape(-1, kv_width)
    value_local = jnp.sum(value_terms, axis=1).transpose(1, 0, 2).reshape(-1, kv_width)
    key_total = key_local[:tok_dev]
    value_total = value_local[:tok_dev]
    for level_index in range(LEVELS):
        row_lower = tok_dev * (level_index + 1)
        outgoing = (
            key_local[row_lower : row_lower + tok_dev],
            value_local[row_lower : row_lower + tok_dev],
        )
        returned = shifted((outgoing[0], outgoing[1]), "ctx", -distances[level_index])
        key_total = key_total + returned[0]
        value_total = value_total + returned[1]
    key_grad, value_grad = (
        lax.all_gather(key_total.astype(jnp.bfloat16), "head", axis=1, tiled=True),
        lax.all_gather(value_total.astype(jnp.bfloat16), "head", axis=1, tiled=True),
    )
    attended = from_grid(out_grid)
    query_grad = from_grid(query_sums.astype(jnp.bfloat16))
    return (attended, query_grad, key_grad, value_grad)


def solution(mesh):
    placed = (P("ctx", "head"), P("ctx", None), P("ctx", None), P("ctx", "head"), P("ctx", None))
    return jax.shard_map(
        local,
        mesh=mesh,
        in_specs=placed,
        out_specs=(P("ctx", "head"), P("ctx", "head"), P("ctx", None), P("ctx", None)),
        check_vma=False,
    )
```

profile of v0, /device:TPU:57, one launch (start us, length us, event | category | flops | bytes accessed | tf_op | source)
XLA Modules:
  0.0 1502.0 jit_solution(12938849226705840808)
XLA Ops:
  14.0 504.2 %all-gather = bf16[256,4,256]{2,1,0:T(4,128)(2,1)S(1)} all-gather(bf16[1,4,256]{2,1,0:T(4,128)(2,1)S(1)} %fusion.258), channel_id=1, replica_groups=mesh['head'=2,'ctx'=256] {'ctx'}, dimensions={0}, use_global_device_ids=true | all-gather | bytes 526336 | tf_op jit(solution)/shard_map/all_gather | solution.py:121
  518.4 564.1 %all-gather.1 = bf16[256,4,256]{2,1,0:T(4,128)(2,1)S(1)} all-gather(bf16[1,4,256]{2,1,0:T(4,128)(2,1)S(1)} %fusion.259), channel_id=1, replica_groups=mesh['head'=2,'ctx'=256] {'ctx'}, dimensions={0}, use_global_device_ids=true | all-gather | bytes 526336 | tf_op jit(solution)/shard_map/all_gather | solution.py:122
  1085.4 6.0 while.159
  1091.4 4.4 while.165
  1095.8 3.8 while.158
  1099.5 2.6 while.164
  1103.1 5.6 while.161
  1104.4 1.5 fusion.347
  1108.8 4.0 while.167
  1108.8 2.0 fusion.389
  1110.8 1.9 fusion.389
  1113.6 3.8 while.160
  1117.4 3.9 while.166
  1117.5 1.9 fusion.385
  1119.4 1.9 fusion.385
  1123.9 13.0 while.163
  1128.0 2.0 fusion.378
  1134.6 1.9 fusion.378
  1137.9 7.8 while.169
  1139.3 2.5 fusion.403
  1143.2 2.5 fusion.403
  1145.7 1.8 reshape_squeeze.15
  1149.3 9.6 while.162
  1159.7 6.0 while.168
  1160.2 2.5 fusion.396
  1163.2 2.5 fusion.396
  1169.7 89.3 %collective-permute-start.7 = (f32[128,256]{0,1:T(8,128)S(1)}, f32[128,256]{0,1:T(8,128)S(1)}, u32[]{:S(2)}, u32[]{:S(2)}) collective-permute-start(f32[128,256]{0,1:T(8,128)S(1)} %bitcast.375), channel_id=1, source_target_pairs={{64,0},{65,1},{66,2},{67,3},{68,4},{69,5},{70,6},{71,7},{72,8},{73... | collective-permute-start | bytes 393224 | tf_op jit(solution)/shard_map/ppermute | solution.py:14
  1259.1 8.4 collective-permute-start.6
  1269.3 1.9 collective-permute-start.10
  1272.5 1.9 collective-permute-start.9
  1274.5 224.0 %all_gather.17 = bf16[128,512]{0,1:T(8,128)(2,1)S(1)} all-gather(bf16[128,256]{0,1:T(8,128)(2,1)S(1)} %fusion.257), channel_id=1, replica_groups=mesh['head'=2,'ctx'=256] {'head'}, dimensions={1}, use_global_device_ids=true | all-gather | bytes 196608 | tf_op jit(solution)/shard_map/all_gather | solution.py:253
  1499.4 1.9 all_gather.18
  (263 shorter events, 69.2 us)
Async XLA Ops:
  0.6 9.8 copy-start.15
  0.6 12.5 copy-start.13
  1.6 1082.2 %collective-permute-start.2 = (bf16[128,256]{1,0:T(8,128)(2,1)S(1)}, bf16[128,256]{1,0:T(8,128)(2,1)S(1)}, u32[]{:S(2)}, u32[]{:S(2)}) collective-permute-start(bf16[128,256]{1,0:T(8,128)(2,1)S(1)} %get-tuple-element.1365), channel_id=1, source_target_pairs={{0,32},{1,33},{2,34},{3,35},{4,36},{5,37},{6,38},{7,39},{8,40},{9,... | collective-permute-start | bytes 196616 | tf_op jit(solution)/shard_map/ppermute | solution.py:14
  2.9 1082.4 %collective-permute-start.1 = (bf16[128,256]{1,0:T(8,128)(2,1)S(1)}, bf16[128,256]{1,0:T(8,128)(2,1)S(1)}, u32[]{:S(2)}, u32[]{:S(2)}) collective-permute-start(bf16[128,256]{1,0:T(8,128)(2,1)S(1)} %get-tuple-element.1365), channel_id=1, source_target_pairs={{0,64},{1,65},{2,66},{3,67},{4,68},{5,69},{6,70},{7,71},{8,72},{9,... | collective-permute-start | bytes 196616 | tf_op jit(solution)/shard_map/ppermute | solution.py:14
  4.2 1081.1 %collective-permute-start = (bf16[128,256]{1,0:T(8,128)(2,1)S(1)}, bf16[128,256]{1,0:T(8,128)(2,1)S(1)}, u32[]{:S(2)}, u32[]{:S(2)}) collective-permute-start(bf16[128,256]{1,0:T(8,128)(2,1)S(1)} %get-tuple-element.1365), channel_id=1, source_target_pairs={{0,128},{1,129},{2,130},{3,131},{4,132},{5,133},{6,134},{7,135},{8... | collective-permute-start | bytes 196616 | tf_op jit(solution)/shard_map/ppermute | solution.py:14
  6.4 1095.8 %collective-permute-start.5 = (bf16[128,256]{1,0:T(8,128)(2,1)S(1)}, bf16[128,256]{1,0:T(8,128)(2,1)S(1)}, u32[]{:S(2)}, u32[]{:S(2)}) collective-permute-start(bf16[128,256]{1,0:T(8,128)(2,1)S(1)} %get-tuple-element.1363), channel_id=1, source_target_pairs={{0,32},{1,33},{2,34},{3,35},{4,36},{5,37},{6,38},{7,39},{8,40},{9,... | collective-permute-start | bytes 196616 | tf_op jit(solution)/shard_map/ppermute | solution.py:14
  7.7 1094.5 %collective-permute-start.4 = (bf16[128,256]{1,0:T(8,128)(2,1)S(1)}, bf16[128,256]{1,0:T(8,128)(2,1)}, u32[]{:S(2)}, u32[]{:S(2)}) collective-permute-start(bf16[128,256]{1,0:T(8,128)(2,1)S(1)} %get-tuple-element.1363), channel_id=1, source_target_pairs={{0,64},{1,65},{2,66},{3,67},{4,68},{5,69},{6,70},{7,71},{8,72},{9,... | collective-permute-start | bytes 196616 | tf_op jit(solution)/shard_map/ppermute | solution.py:14
  13.1 1070.3 %copy-start.14 = (bf16[128,2048]{1,0:T(8,128)(2,1)S(1)}, bf16[128,2048]{1,0:T(8,128)(2,1)}, u32[]{:S(2)}) copy-start(bf16[128,2048]{1,0:T(8,128)(2,1)} %param.32) | copy-start | bytes 1572868
  1083.8 18.4 %collective-permute-start.3 = (bf16[128,256]{1,0:T(8,128)(2,1)S(1)}, bf16[128,256]{1,0:T(8,128)(2,1)}, u32[]{:S(2)}, u32[]{:S(2)}) collective-permute-start(bf16[128,256]{1,0:T(8,128)(2,1)S(1)} %get-tuple-element.1363), channel_id=1, source_target_pairs={{0,128},{1,129},{2,130},{3,131},{4,132},{5,133},{6,134},{7,135},{8... | collective-permute-start | bytes 196616 | tf_op jit(solution)/shard_map/ppermute | solution.py:14
  1121.3 2.6 copy-start.4
  1136.9 0.7 copy-start
  1136.9 0.8 copy-start.2
  1136.9 1.0 copy-start.8
  1145.7 3.6 copy-start.1
  1145.7 3.6 copy-start.3
  1145.7 3.6 copy-start.5
  1158.9 0.8 copy-start.6
  1165.7 102.0 %copy-start.7 = (f32[2,512,128]{2,1,0:T(8,128)S(1)}, f32[2,512,128]{2,1,0:T(8,128)}, u32[]{:S(2)}) copy-start(f32[2,512,128]{2,1,0:T(8,128)} %copy-done.6) | copy-start | bytes 1572868
  1165.7 102.0 %copy-start.9 = (f32[2,512,128]{2,1,0:T(8,128)S(1)}, f32[2,512,128]{2,1,0:T(8,128)}, u32[]{:S(2)}) copy-start(f32[2,512,128]{2,1,0:T(8,128)} %copy-done.8) | copy-start | bytes 1572868
  1168.3 104.2 %collective-permute-start.8 = (f32[128,256]{0,1:T(8,128)S(1)}, f32[128,256]{0,1:T(8,128)S(1)}, u32[]{:S(2)}, u32[]{:S(2)}) collective-permute-start(f32[128,256]{0,1:T(8,128)S(1)} %bitcast.376), channel_id=1, source_target_pairs={{32,0},{33,1},{34,2},{35,3},{36,4},{37,5},{38,6},{39,7},{40,8},{41... | collective-permute-start | bytes 393224 | tf_op jit(solution)/shard_map/ppermute | solution.py:14
  1169.7 104.7 %collective-permute-start.7 = (f32[128,256]{0,1:T(8,128)S(1)}, f32[128,256]{0,1:T(8,128)S(1)}, u32[]{:S(2)}, u32[]{:S(2)}) collective-permute-start(f32[128,256]{0,1:T(8,128)S(1)} %bitcast.375), channel_id=1, source_target_pairs={{64,0},{65,1},{66,2},{67,3},{68,4},{69,5},{70,6},{71,7},{72,8},{73... | collective-permute-start | bytes 393224 | tf_op jit(solution)/shard_map/ppermute | solution.py:14
  1259.0 12.5 copy-start.10
  1259.0 12.5 copy-start.11
  1259.0 12.5 copy-start.12
  1259.1 15.3 %collective-permute-start.6 = (f32[128,256]{0,1:T(8,128)S(1)}, f32[128,256]{0,1:T(8,128)S(1)}, u32[]{:S(2)}, u32[]{:S(2)}) collective-permute-start(f32[128,256]{0,1:T(8,128)S(1)} %bitcast.377), channel_id=1, source_target_pairs={{128,0},{129,1},{130,2},{131,3},{132,4},{133,5},{134,6},{135,7},{1... | collective-permute-start | bytes 393224 | tf_op jit(solution)/shard_map/ppermute | solution.py:14
  1267.9 231.4 %collective-permute-start.11 = (f32[128,256]{0,1:T(8,128)S(1)}, f32[128,256]{0,1:T(8,128)S(1)}, u32[]{:S(2)}, u32[]{:S(2)}) collective-permute-start(f32[128,256]{0,1:T(8,128)S(1)} %bitcast.378), channel_id=1, source_target_pairs={{32,0},{33,1},{34,2},{35,3},{36,4},{37,5},{38,6},{39,7},{40,8},{41... | collective-permute-start | bytes 393224 | tf_op jit(solution)/shard_map/ppermute | solution.py:14
  1269.3 230.0 %collective-permute-start.10 = (f32[128,256]{0,1:T(8,128)S(1)}, f32[128,256]{0,1:T(8,128)S(1)}, u32[]{:S(2)}, u32[]{:S(2)}) collective-permute-start(f32[128,256]{0,1:T(8,128)S(1)} %bitcast.379), channel_id=1, source_target_pairs={{64,0},{65,1},{66,2},{67,3},{68,4},{69,5},{70,6},{71,7},{72,8},{73... | collective-permute-start | bytes 393224 | tf_op jit(solution)/shard_map/ppermute | solution.py:14
  1272.5 226.8 %collective-permute-start.9 = (f32[128,256]{0,1:T(8,128)S(1)}, f32[128,256]{0,1:T(8,128)S(1)}, u32[]{:S(2)}, u32[]{:S(2)}) collective-permute-start(f32[128,256]{0,1:T(8,128)S(1)} %bitcast.380), channel_id=1, source_target_pairs={{128,0},{129,1},{130,2},{131,3},{132,4},{133,5},{134,6},{135,7},{1... | collective-permute-start | bytes 393224 | tf_op jit(solution)/shard_map/ppermute | solution.py:14
where the time goes:
time: 1510 us; the launch traced here: 1500 us
  blocking collectives  1290 us (85%)
  starting transfers between devices  112 us (7%)
  matrix products  49.1 us (3%)
  local copies, waits for them, and re-layouts  24.9 us (2%)
    all_gather x1, blocking collectives, land_pass(): lax.all_gather(land_values, 'ctx', axis=0, tiled=True)  564 us
    all_gather x1, blocking collectives, land_pass(): lax.all_gather(land_keys, 'ctx', axis=0, tiled=True)  504 us
    all_gather x1, blocking collectives, local(): lax.all_gather(key_total.astype(jnp.bfloat16), 'head', axis=1, tiled=True)  224 us
    ppermute x12, starting transfers between devices, shifted(): lax.ppermute(value, axis, [(source, source + steps) for source in range(l...  112 us
  transfers between devices with their start and end apart: 12, of which 0 were waited for; matrix products, arithmetic and copies ran while one was open for 1% of the time, Pallas kernels for 0%

commit v1 on v0

v1 whole, which is shorter than its diff:
```python
import functools

import jax
import jax.numpy as jnp
from jax import lax
from jax.experimental import pallas as pl
from jax.experimental.pallas import tpu as pltpu
from jax.sharding import PartitionSpec as P

HD = 128
POOL = 32
LEVELS = 3
TOK = 128
CHUNK = 256
BIG = -1e30
SCALE = HD**-0.5
LOG2E = 1.4426950408889634
F32 = jnp.float32
BF16 = jnp.bfloat16
NT = (((1,), (1,)), ((), ()))
NN = (((1,), (0,)), ((), ()))
TN = (((0,), (0,)), ((), ()))

FIRST = [
    [(2 * yk + yb) * 32 + x * 8 + 2 * zk + zb for yk in range(4) for zk in range(4)]
    for yb in range(2)
    for x in range(4)
    for zb in range(2)
]
SECOND = [
    [(2 * yk + yb) * 32 + x * 8 + 2 * zk + zb for yb in range(2) for x in range(4) for zb in range(2)]
    for yk in range(4)
    for zk in range(4)
]


def mul(a, b, dims):
    return lax.dot_general(a, b, dims, preferred_element_type=F32)


def pool_kernel(key_ref, value_ref, kv_ref, land_ref):
    col = pl.multiple_of(lax.axis_index("head") * 256, 256)
    parts = []
    for ref, low in ((key_ref, 0), (value_ref, 256)):
        rows = ref[:, pl.ds(col, 256)]
        kv_ref[:, low : low + 256] = rows
        wide = rows.astype(F32)
        parts.append(
            jnp.concatenate(
                [jnp.sum(wide[j * POOL : (j + 1) * POOL], axis=0, keepdims=True) for j in range(TOK // POOL)],
                axis=0,
            )
            * (1.0 / POOL)
        )
    land = jnp.concatenate(parts, axis=1)
    copies = land_ref.shape[0] // land.shape[0]
    land_ref[...] = jnp.concatenate([land] * copies, axis=0).astype(BF16)


def pool(key_rows, value_rows):
    return pl.pallas_call(
        pool_kernel,
        out_shape=(
            jax.ShapeDtypeStruct((TOK, 512), BF16),
            jax.ShapeDtypeStruct((4 * len(FIRST[0]), 512), BF16),
        ),
    )(key_rows, value_rows)


def land_block(row):
    first = (row >> 2) & 15
    second = row >> 6
    y = ((first >> 2) << 1) | (second >> 3)
    x = (second >> 1) & 3
    z = ((first & 3) << 1) | (second & 1)
    return y * 32 + x * 8 + z


def attend_kernel(
    ctx_count,
    keep_ref,
    q_ref,
    do_ref,
    own_ref,
    p0_ref,
    p1_ref,
    p2_ref,
    land_ref,
    att_ref,
    dq_ref,
    own_grad_ref,
    g0_ref,
    g1_ref,
    g2_ref,
    keys,
    values,
    work,
    dk,
    dv,
):
    step = pl.program_id(0)
    block = lax.axis_index("ctx")
    partners = (p0_ref, p1_ref, p2_ref)
    n_keys = keys.shape[0]
    n_local = TOK * (1 + LEVELS)

    @pl.when(step == 0)
    def _():
        row = lax.broadcasted_iota(jnp.int32, (TOK, TOK), 0)
        col = lax.broadcasted_iota(jnp.int32, (TOK, TOK), 1)
        keys[:TOK, HD:] = jnp.where(row > col, BIG, 0.0).astype(BF16)
        for level in range(LEVELS):
            distance = ctx_count // 2 ** (level + 1)
            wanted = jnp.logical_and((block // distance) % 2 == 1, keep_ref[0, level] == 1)
            bias = jnp.where(wanted, 0.0, BIG)
            keys[TOK * (level + 1) : TOK * (level + 2), HD:] = jnp.full((TOK, HD), bias, F32).astype(BF16)
        row = lax.broadcasted_iota(jnp.int32, (n_keys - n_local, HD), 0)
        keys[n_local:, HD:] = jnp.where(land_block(row) < block, 0.0, BIG).astype(BF16)

    for head in range(2):

        @pl.when(step == 4 * head)
        def _():
            k_cols = slice(head * HD, (head + 1) * HD)
            v_cols = slice(256 + head * HD, 256 + (head + 1) * HD)
            for number, ref in enumerate((own_ref,) + partners):
                keys[number * TOK : (number + 1) * TOK, :HD] = ref[:, k_cols]
                values[number * TOK : (number + 1) * TOK, :] = ref[:, v_cols]
            keys[n_local:, :HD] = land_ref[:, k_cols]
            values[n_local:, :] = land_ref[:, v_cols]
            dk[...] = jnp.zeros_like(dk)
            dv[...] = jnp.zeros_like(dv)

    q = jnp.concatenate([q_ref[:, :HD], q_ref[:, HD:]], axis=0)
    do = jnp.concatenate([do_ref[:, :HD], do_ref[:, HD:]], axis=0)
    rows = q.shape[0]
    token = lax.broadcasted_iota(jnp.int32, (rows, HD), 0) & (TOK - 1)
    pick = jnp.where(token == lax.broadcasted_iota(jnp.int32, (rows, HD), 1), 1.0, 0.0)
    q_pick = jnp.concatenate([q, pick.astype(BF16)], axis=1)
    chunks = [slice(low, low + CHUNK) for low in range(0, n_keys, CHUNK)]

    peak = None
    for chunk in chunks:
        score = mul(q_pick, keys[chunk, :], NT) * (SCALE * LOG2E)
        work[:, chunk] = score
        for low in range(0, CHUNK, 128):
            piece = score[:, low : low + 128]
            peak = piece if peak is None else jnp.maximum(peak, piece)
    peak = jnp.max(peak, axis=1, keepdims=True)
    total = None
    for chunk in chunks:
        prob = jnp.exp2(work[:, chunk] - peak)
        work[:, chunk] = prob
        for low in range(0, CHUNK, 128):
            piece = prob[:, low : low + 128]
            total = piece if total is None else total + piece
    inverse = 1.0 / jnp.sum(total, axis=1, keepdims=True)
    out = None
    for number, chunk in enumerate(chunks):
        soft = work[:, chunk] * inverse
        work[:, chunk] = soft
        half = soft.astype(BF16)
        term = mul(half, values[chunk, :], NN)
        out = term if out is None else out + term
        if number < n_local // CHUNK:
            dv[chunk, :] += mul(half, do, TN)
    out = out.astype(BF16)
    att_ref[:, :HD] = out[:TOK]
    att_ref[:, HD:] = out[TOK:]
    delta = jnp.sum(do.astype(F32) * out.astype(F32), axis=1, keepdims=True)
    dq = None
    for number, chunk in enumerate(chunks):
        dsoft = mul(do, values[chunk, :], NT)
        dscore = (work[:, chunk] * (dsoft - delta)).astype(BF16)
        term = mul(dscore, keys[chunk, :HD], NN)
        dq = term if dq is None else dq + term
        if number < n_local // CHUNK:
            dk[chunk, :] += mul(dscore, q, TN)
    dq = (SCALE * dq).astype(BF16)
    dq_ref[:, :HD] = dq[:TOK]
    dq_ref[:, HD:] = dq[TOK:]

    for head in range(2):

        @pl.when(step == 4 * head + 3)
        def _():
            for source, factor, low in ((dk, SCALE, head * HD), (dv, 1.0, 256 + head * HD)):
                own_grad_ref[:, low : low + HD] = source[:TOK, :] * factor
                for level, ref in enumerate((g0_ref, g1_ref, g2_ref)):
                    part = source[TOK * (level + 1) : TOK * (level + 2), :] * factor
                    ref[:, low : low + HD] = part.astype(BF16)


def attend(ctx_count, partner_keep, queries, out_grad, own, partners, land):
    n_keys = TOK * (1 + LEVELS) + land.shape[0]
    wide = pl.BlockSpec((TOK, 256), lambda i: (0, i))
    whole = pl.BlockSpec((TOK, 512), lambda i: (0, 0))
    return pl.pallas_call(
        functools.partial(attend_kernel, ctx_count),
        grid=(8,),
        in_specs=[
            pl.BlockSpec(memory_space=pltpu.SMEM),
            wide,
            wide,
            whole,
            whole,
            whole,
            whole,
            pl.BlockSpec(land.shape, lambda i: (0, 0)),
        ],
        out_specs=[wide, wide, whole, whole, whole, whole],
        out_shape=[
            jax.ShapeDtypeStruct((TOK, 2048), BF16),
            jax.ShapeDtypeStruct((TOK, 2048), BF16),
            jax.ShapeDtypeStruct((TOK, 512), F32),
        ]
        + [jax.ShapeDtypeStruct((TOK, 512), BF16)] * LEVELS,
        scratch_shapes=[
            pltpu.VMEM((n_keys, 2 * HD), BF16),
            pltpu.VMEM((n_keys, HD), BF16),
            pltpu.VMEM((256, n_keys), F32),
            pltpu.VMEM((TOK * (1 + LEVELS), HD), F32),
            pltpu.VMEM((TOK * (1 + LEVELS), HD), F32),
        ],
        compiler_params=pltpu.CompilerParams(vmem_limit_bytes=32 * 2**20),
    )(partner_keep, queries, out_grad, own, *partners, land)


def total_kernel(own_ref, r0_ref, r1_ref, r2_ref, sum_ref):
    total = own_ref[...]
    for ref in (r0_ref, r1_ref, r2_ref):
        total = total + ref[...].astype(F32)
    sum_ref[...] = total.astype(BF16)


def exchange(rows, groups):
    return lax.all_to_all(rows, "ctx", 0, 0, axis_index_groups=groups, tiled=True)


def local(queries, key_rows, value_rows, out_grad, partner_keep):
    ctx_count = lax.axis_size("ctx")
    own, land = pool(key_rows, value_rows)
    pairs = []
    for level in range(LEVELS):
        distance = ctx_count // 2 ** (level + 1)
        pairs.append([(b, b + distance) for b in range(ctx_count) if b // distance % 2 == 0])
    partners = [lax.ppermute(own, "ctx", pair) for pair in pairs]
    land = exchange(land, FIRST)
    land = jnp.broadcast_to(land[None], (len(SECOND[0]),) + land.shape)
    land = exchange(land, SECOND).reshape(-1, 512)
    att, dq, own_grad, *sent = attend(ctx_count, partner_keep, queries, out_grad, own, partners, land)
    back = [
        lax.ppermute(part, "ctx", [(later, earlier) for earlier, later in pair]) for part, pair in zip(sent, pairs)
    ]
    total = pl.pallas_call(total_kernel, out_shape=jax.ShapeDtypeStruct((TOK, 512), BF16))(own_grad, *back)
    both = lax.all_gather(total, "head", axis=0)
    key_grad = jnp.concatenate([both[0, :, :256], both[1, :, :256]], axis=1)
    value_grad = jnp.concatenate([both[0, :, 256:], both[1, :, 256:]], axis=1)
    return att, dq, key_grad, value_grad


def solution(mesh):
    placed = (P("ctx", "head"), P("ctx", None), P("ctx", None), P("ctx", "head"), P("ctx", None))
    return jax.shard_map(
        local,
        mesh=mesh,
        in_specs=placed,
        out_specs=(P("ctx", "head"), P("ctx", "head"), P("ctx", None), P("ctx", None)),
        check_vma=False,
    )
```

time: 1510 us -> 93.8 us (0.06)
  blocking collectives: 1290 us -> 28.1 us
  starting transfers between devices: 112 us -> 22.3 us
  matrix products: 49.1 us -> 0 us
  local copies, waits for them, and re-layouts: 24.9 us -> 3.33 us
  Pallas kernels: 0 us -> 21.1 us
  waiting for transfers between devices: 0.03 us -> 15.8 us
    all_gather x4 -> x1, blocking collectives: 1290 us -> 4.94 us  [local(): both = lax.all_gather(total, 'head', axis=0)]
    ppermute x12 -> x6, starting transfers between devices: 112 us -> 15.8 us  [the longest x3 11.9 us: local(): lax.ppermute(part, 'ctx', [(later, earlier) for earlier, later in pair])]
    dot_general x44 -> x0, matrix products: 49.1 us -> none  [the longest x16 14.6 us: masked_scores(): jnp.einsum('rd,kd->rk', query_rows, key_block, preferred_element_type=jnp...]
    all_to_all x0 -> x1, blocking collectives: none -> 23.2 us  [exchange(): lax.all_to_all(rows, 'ctx', 0, 0, axis_index_groups=groups, tiled=True)]
    pallas_call x0 -> x3, Pallas kernels: none -> 21.1 us  [the longest x1 17.6 us: attend(): pl.pallas_call(functools.partial(attend_kernel, ctx_count), grid=(8,), in...]
    ppermute x12 -> x6, waiting for transfers between devices: 0.03 us -> 15.8 us  [the longest x3 12.6 us: local(): partners = [lax.ppermute(own, 'ctx', pair) for pair in pairs]]
  transfers between devices with their start and end apart: 12 -> 7, of which waited for: 0 -> 3; matrix products, arithmetic and copies ran while one was open for 1% -> 0% of each run, Pallas kernels for 0% -> 0%
where the time goes in v1:
time: 93.8 us; the launch traced here: 92.1 us
  blocking collectives  28.1 us (30%)
  starting transfers between devices  22.3 us (24%)
  Pallas kernels  21.1 us (22%)
  waiting for transfers between devices  15.8 us (17%)
  local copies, waits for them, and re-layouts  3.33 us (4%)
    all_to_all x1, blocking collectives, exchange(): lax.all_to_all(rows, 'ctx', 0, 0, axis_index_groups=groups, tiled=True)  23.2 us
    pallas_call x1, Pallas kernels, attend(): pl.pallas_call(functools.partial(attend_kernel, ctx_count), grid=(8,), in...  17.6 us
    ppermute x3, waiting for transfers between devices, local(): partners = [lax.ppermute(own, 'ctx', pair) for pair in pairs]  12.6 us
    ppermute x3, starting transfers between devices, local(): lax.ppermute(part, 'ctx', [(later, earlier) for earlier, later in pair])  11.9 us
    all_to_all x1, starting transfers between devices, exchange(): lax.all_to_all(rows, 'ctx', 0, 0, axis_index_groups=groups, tiled=True)  6.5 us
    all_gather x1, blocking collectives, local(): both = lax.all_gather(total, 'head', axis=0)  4.94 us
    ppermute x3, starting transfers between devices, local(): partners = [lax.ppermute(own, 'ctx', pair) for pair in pairs]  3.88 us
    ppermute x3, waiting for transfers between devices, local(): lax.ppermute(part, 'ctx', [(later, earlier) for earlier, later in pair])  3.21 us
  transfers between devices with their start and end apart: 7, of which 3 were waited for; matrix products, arithmetic and copies ran while one was open for 0% of the time, Pallas kernels for 0%

profile of v1, /device:TPU:57, one launch (start us, length us, event | category | flops | bytes accessed | tf_op | source)
XLA Modules:
  0.0 92.1 jit_solution(4022492108353552808)
XLA Ops:
  0.6 1.7 %shard_map.84 = (bf16[128,512]{1,0:T(8,128)(2,1)}, bf16[64,512]{1,0:T(8,128)(2,1)}) custom-call(bf16[128,512]{1,0:T(8,128)(2,1)} %key_ref.1, bf16[128,512]{1,0:T(8,128)(2,1)} %value_ref.1), custom_call_target="tpu_custom_call" | custom-call | tf_op jit(solution)/shard_map/pallas_call | solution.py:61
  2.3 0.9 all_to_all.9
  3.1 23.2 %all_to_all.14 = bf16[16,4,512]{2,1,0:T(4,128)(2,1)S(1)} all-to-all(bf16[16,4,512]{2,1,0:T(4,128)(2,1)S(1)} %all_to_all.9), channel_id=1, replica_groups={{0,2,4,6,64,66,68,70,128,130,132,134,192,194,196,198},{1,3,5,7,65,67,69..., dimensions={0} | all-to-all | bytes 131072 | tf_op jit(solution)/shard_map/all_to_all | solution.py:237
  26.4 1.1 %broadcast_in_dim.9 = bf16[16,64,512]{2,1,0:T(8,128)(2,1)} broadcast(bf16[64,512]{1,0:T(8,128)(2,1)S(1)} %broadcast_in_dim.8), dimensions={1,2} | broadcast | bytes 1114112 | tf_op jit(solution)/shard_map/broadcast_in_dim | solution.py:249
  27.5 6.5 %all-to-all-start.1 = ((bf16[16,64,512]{2,1,0:T(8,128)(2,1)}), bf16[16,64,512]{2,1,0:T(8,128)(2,1)S(1)}, u32[]{:S(2)}, u32[]{:S(2)}) async-start(bf16[16,64,512]{2,1,0:T(8,128)(2,1)} %broadcast_in_dim.9), calls=%async_computation.1 | async-start | bytes 2097152 | tf_op jit(solution)/shard_map/all_to_all | solution.py:237
  34.0 0.0 copy-done.3
  34.0 0.0 copy-start.4
  34.0 1.3 %collective-permute-start.2 = (bf16[128,512]{1,0:T(8,128)(2,1)S(1)}, bf16[128,512]{1,0:T(8,128)(2,1)S(1)}, u32[]{:S(2)}, u32[]{:S(2)}) collective-permute-start(bf16[128,512]{1,0:T(8,128)(2,1)S(1)} %copy-done.3), channel_id=1, source_target_pairs={{0,32},{1,33},{2,34},{3,35},{4,36},{5,37},{6,38},{7,39},{8,40},{9,... | collective-permute-start | bytes 393224 | tf_op jit(solution)/shard_map/ppermute | solution.py:247
  35.3 1.3 %collective-permute-start.1 = (bf16[128,512]{1,0:T(8,128)(2,1)S(1)}, bf16[128,512]{1,0:T(8,128)(2,1)S(1)}, u32[]{:S(2)}, u32[]{:S(2)}) collective-permute-start(bf16[128,512]{1,0:T(8,128)(2,1)S(1)} %copy-done.3), channel_id=1, source_target_pairs={{0,64},{1,65},{2,66},{3,67},{4,68},{5,69},{6,70},{7,71},{8,72},{9,... | collective-permute-start | bytes 393224 | tf_op jit(solution)/shard_map/ppermute | solution.py:247
  36.6 1.3 %collective-permute-start = (bf16[128,512]{1,0:T(8,128)(2,1)S(1)}, bf16[128,512]{1,0:T(8,128)(2,1)S(1)}, u32[]{:S(2)}, u32[]{:S(2)}) collective-permute-start(bf16[128,512]{1,0:T(8,128)(2,1)S(1)} %copy-done.3), channel_id=1, source_target_pairs={{0,128},{1,129},{2,130},{3,131},{4,132},{5,133},{6,134},{7,135},{8... | collective-permute-start | bytes 393224 | tf_op jit(solution)/shard_map/ppermute | solution.py:247
  37.9 12.1 %collective-permute-done.2.p2_ref = bf16[128,512]{1,0:T(8,128)(2,1)S(1)} collective-permute-done((bf16[128,512]{1,0:T(8,128)(2,1)S(1)}, bf16[128,512]{1,0:T(8,128)(2,1)S(1)}, u32[]{:S(2)}, u32[]{:S(2)}) %collective-permute-start.2) | collective-permute-done | bytes 131104 | tf_op jit(solution)/shard_map/ppermute | solution.py:247
  50.0 0.0 collective-permute-done.1.p1_ref
  50.0 0.5 collective-permute-done.p0_ref
  50.4 0.0 all-to-all-done.1
  50.4 0.0 copy-done
  50.4 0.0 copy-done.1
  50.5 0.0 copy-done.4
  50.5 17.6 %shard_map.85 = (bf16[128,2048]{1,0:T(8,128)(2,1)}, bf16[128,2048]{1,0:T(8,128)(2,1)}, f32[128,512]{1,0:T(8,128)S(1)}, bf16[128,512]{1,0:T(8,128)(2,1)S(1)}, bf1...) custom-call(s32[1,3]{1,0:T(1,128)S(1)} %copy-done.4, bf16[128,2048]{1,0:T(8,128)(2,1)S(1)} %copy-done, ...), custom_call_target="tpu_custom_call" | custom-call | tf_op jit(solution)/shard_map/pallas_call | solution.py:198
  68.1 0.7 copy-done.2
  68.8 4.2 %collective-permute-start.3 = (bf16[128,512]{1,0:T(8,128)(2,1)S(1)}, bf16[128,512]{1,0:T(8,128)(2,1)S(1)}, u32[]{:S(2)}, u32[]{:S(2)}) collective-permute-start(bf16[128,512]{1,0:T(8,128)(2,1)S(1)} %get-tuple-element.17), channel_id=1, source_target_pairs={{128,0},{129,1},{130,2},{131,3},{132,4},{133,5},{134,6},{135,7},{1... | collective-permute-start | bytes 393224 | tf_op jit(solution)/shard_map/ppermute | solution.py:253
  73.0 3.3 %collective-permute-start.4 = (bf16[128,512]{1,0:T(8,128)(2,1)S(1)}, bf16[128,512]{1,0:T(8,128)(2,1)S(1)}, u32[]{:S(2)}, u32[]{:S(2)}) collective-permute-start(bf16[128,512]{1,0:T(8,128)(2,1)S(1)} %get-tuple-element.18), channel_id=1, source_target_pairs={{64,0},{65,1},{66,2},{67,3},{68,4},{69,5},{70,6},{71,7},{72,8},{73... | collective-permute-start | bytes 393224 | tf_op jit(solution)/shard_map/ppermute | solution.py:253
  76.3 4.4 %collective-permute-start.5 = (bf16[128,512]{1,0:T(8,128)(2,1)S(1)}, bf16[128,512]{1,0:T(8,128)(2,1)S(1)}, u32[]{:S(2)}, u32[]{:S(2)}) collective-permute-start(bf16[128,512]{1,0:T(8,128)(2,1)S(1)} %get-tuple-element.19), channel_id=1, source_target_pairs={{32,0},{33,1},{34,2},{35,3},{36,4},{37,5},{38,6},{39,7},{40,8},{41... | collective-permute-start | bytes 393224 | tf_op jit(solution)/shard_map/ppermute | solution.py:253
  80.7 0.0 collective-permute-done.3.r0_ref
  80.7 0.0 copy-start.5
  80.8 0.0 collective-permute-done.4.r1_ref
  80.8 0.0 copy-start.6
  80.8 3.2 %collective-permute-done.5.r2_ref = bf16[128,512]{1,0:T(8,128)(2,1)S(1)} collective-permute-done((bf16[128,512]{1,0:T(8,128)(2,1)S(1)}, bf16[128,512]{1,0:T(8,128)(2,1)S(1)}, u32[]{:S(2)}, u32[]{:S(2)}) %collective-permute-start.5) | collective-permute-done | bytes 131104 | tf_op jit(solution)/shard_map/ppermute | solution.py:253
  84.0 0.0 copy-done.5
  84.0 0.6 copy-done.7
  84.6 1.8 %shard_map.86 = bf16[128,512]{1,0:T(8,128)(2,1)} custom-call(f32[128,512]{1,0:T(8,128)} %copy-done.2, bf16[128,512]{1,0:T(8,128)(2,1)} %copy-done.5, bf16[128,512]{1,0:T(8,128)(2,1)} %copy-done.6, bf16[128,512]{1,0:T(8,128)(2,1)} %copy-done.7), custom_call_target="tpu_custom_call" | custom-call | tf_op jit(solution)/shard_map/pallas_call | solution.py:255
  86.4 4.9 %all-gather = bf16[256,512]{1,0:T(8,128)(2,1)S(1)} all-gather(bf16[128,512]{1,0:T(8,128)(2,1)} %shard_map.86), channel_id=2, replica_groups=mesh['head'=2,'ctx'=256] {'head'}, dimensions={0}, use_global_device_ids=true | all-gather | bytes 393216 | tf_op jit(solution)/shard_map/all_gather | solution.py:256
  91.4 0.7 pad_maximum_fusion
  (8 shorter events, 0.0 us)
Async XLA Ops:
  27.5 6.5 %copy-start.3 = (bf16[128,512]{1,0:T(8,128)(2,1)S(1)}, bf16[128,512]{1,0:T(8,128)(2,1)}, u32[]{:S(2)}) copy-start(bf16[128,512]{1,0:T(8,128)(2,1)} %get-tuple-element.12.own_ref) | copy-start | bytes 393220
  27.5 23.0 %copy-start = (bf16[128,2048]{1,0:T(8,128)(2,1)S(1)}, bf16[128,2048]{1,0:T(8,128)(2,1)}, u32[]{:S(2)}) copy-start(bf16[128,2048]{1,0:T(8,128)(2,1)} %q_ref.1) | copy-start | bytes 1572868
  27.5 23.0 %copy-start.1 = (bf16[128,2048]{1,0:T(8,128)(2,1)S(1)}, bf16[128,2048]{1,0:T(8,128)(2,1)}, u32[]{:S(2)}) copy-start(bf16[128,2048]{1,0:T(8,128)(2,1)} %do_ref.1) | copy-start | bytes 1572868
  27.5 23.0 %all-to-all-start.1 = ((bf16[16,64,512]{2,1,0:T(8,128)(2,1)}), bf16[16,64,512]{2,1,0:T(8,128)(2,1)S(1)}, u32[]{:S(2)}, u32[]{:S(2)}) async-start(bf16[16,64,512]{2,1,0:T(8,128)(2,1)} %broadcast_in_dim.9), calls=%async_computation.1 | async-start | bytes 2097152 | tf_op jit(solution)/shard_map/all_to_all | solution.py:237
  34.0 16.5 %copy-start.4 = (s32[1,3]{1,0:T(1,128)S(1)}, s32[1,3]{1,0:T(1,128)}, u32[]{:S(2)}) copy-start(s32[1,3]{1,0:T(1,128)} %keep_ref.1) | copy-start | bytes 40
  34.0 16.0 %collective-permute-start.2 = (bf16[128,512]{1,0:T(8,128)(2,1)S(1)}, bf16[128,512]{1,0:T(8,128)(2,1)S(1)}, u32[]{:S(2)}, u32[]{:S(2)}) collective-permute-start(bf16[128,512]{1,0:T(8,128)(2,1)S(1)} %copy-done.3), channel_id=1, source_target_pairs={{0,32},{1,33},{2,34},{3,35},{4,36},{5,37},{6,38},{7,39},{8,40},{9,... | collective-permute-start | bytes 393224 | tf_op jit(solution)/shard_map/ppermute | solution.py:247
  35.3 14.7 %collective-permute-start.1 = (bf16[128,512]{1,0:T(8,128)(2,1)S(1)}, bf16[128,512]{1,0:T(8,128)(2,1)S(1)}, u32[]{:S(2)}, u32[]{:S(2)}) collective-permute-start(bf16[128,512]{1,0:T(8,128)(2,1)S(1)} %copy-done.3), channel_id=1, source_target_pairs={{0,64},{1,65},{2,66},{3,67},{4,68},{5,69},{6,70},{7,71},{8,72},{9,... | collective-permute-start | bytes 393224 | tf_op jit(solution)/shard_map/ppermute | solution.py:247
  36.6 13.9 %collective-permute-start = (bf16[128,512]{1,0:T(8,128)(2,1)S(1)}, bf16[128,512]{1,0:T(8,128)(2,1)S(1)}, u32[]{:S(2)}, u32[]{:S(2)}) collective-permute-start(bf16[128,512]{1,0:T(8,128)(2,1)S(1)} %copy-done.3), channel_id=1, source_target_pairs={{0,128},{1,129},{2,130},{3,131},{4,132},{5,133},{6,134},{7,135},{8... | collective-permute-start | bytes 393224 | tf_op jit(solution)/shard_map/ppermute | solution.py:247
  68.1 0.7 copy-start.2
  68.8 11.9 %collective-permute-start.3 = (bf16[128,512]{1,0:T(8,128)(2,1)S(1)}, bf16[128,512]{1,0:T(8,128)(2,1)S(1)}, u32[]{:S(2)}, u32[]{:S(2)}) collective-permute-start(bf16[128,512]{1,0:T(8,128)(2,1)S(1)} %get-tuple-element.17), channel_id=1, source_target_pairs={{128,0},{129,1},{130,2},{131,3},{132,4},{133,5},{134,6},{135,7},{1... | collective-permute-start | bytes 393224 | tf_op jit(solution)/shard_map/ppermute | solution.py:253
  73.0 7.7 %collective-permute-start.4 = (bf16[128,512]{1,0:T(8,128)(2,1)S(1)}, bf16[128,512]{1,0:T(8,128)(2,1)S(1)}, u32[]{:S(2)}, u32[]{:S(2)}) collective-permute-start(bf16[128,512]{1,0:T(8,128)(2,1)S(1)} %get-tuple-element.18), channel_id=1, source_target_pairs={{64,0},{65,1},{66,2},{67,3},{68,4},{69,5},{70,6},{71,7},{72,8},{73... | collective-permute-start | bytes 393224 | tf_op jit(solution)/shard_map/ppermute | solution.py:253
  76.3 7.6 %collective-permute-start.5 = (bf16[128,512]{1,0:T(8,128)(2,1)S(1)}, bf16[128,512]{1,0:T(8,128)(2,1)S(1)}, u32[]{:S(2)}, u32[]{:S(2)}) collective-permute-start(bf16[128,512]{1,0:T(8,128)(2,1)S(1)} %get-tuple-element.19), channel_id=1, source_target_pairs={{32,0},{33,1},{34,2},{35,3},{36,4},{37,5},{38,6},{39,7},{40,8},{41... | collective-permute-start | bytes 393224 | tf_op jit(solution)/shard_map/ppermute | solution.py:253
  80.7 3.2 %copy-start.5 = (bf16[128,512]{1,0:T(8,128)(2,1)}, bf16[128,512]{1,0:T(8,128)(2,1)S(1)}, u32[]{:S(2)}) copy-start(bf16[128,512]{1,0:T(8,128)(2,1)S(1)} %collective-permute-done.3.r0_ref) | copy-start | bytes 393220
  80.8 3.2 %copy-start.6 = (bf16[128,512]{1,0:T(8,128)(2,1)}, bf16[128,512]{1,0:T(8,128)(2,1)S(1)}, u32[]{:S(2)}) copy-start(bf16[128,512]{1,0:T(8,128)(2,1)S(1)} %collective-permute-done.4.r1_ref) | copy-start | bytes 393220
  84.0 0.6 copy-start.7

commit v2 on v1

v2 whole, which is shorter than its diff:
```python
import functools

import jax
import jax.numpy as jnp
from jax import lax
from jax.experimental import pallas as pl
from jax.experimental.pallas import tpu as pltpu
from jax.sharding import PartitionSpec as P

HD = 128
POOL = 32
LEVELS = 3
TOK = 128
CHUNK = 256
BIG = -1e30
SCALE = HD**-0.5
LOG2E = 1.4426950408889634
F32 = jnp.float32
BF16 = jnp.bfloat16
NT = (((1,), (1,)), ((), ()))
NN = (((1,), (0,)), ((), ()))
TN = (((0,), (0,)), ((), ()))

FIRST = [[y * 32 + x * 8 + z for y in range(8) for z in range(8)] for x in range(4)]
SECOND = [[y * 32 + x * 8 + z for x in range(4)] for y in range(8) for z in range(8)]


def mul(a, b, dims):
    return lax.dot_general(a, b, dims, preferred_element_type=F32)


def pool_kernel(key_ref, value_ref, kv_ref, land_ref):
    col = pl.multiple_of(lax.axis_index("head") * 256, 256)
    parts = []
    for ref, low in ((key_ref, 0), (value_ref, 256)):
        rows = ref[:, pl.ds(col, 256)]
        kv_ref[:, low : low + 256] = rows
        wide = rows.astype(F32)
        parts.append(
            jnp.concatenate(
                [jnp.sum(wide[j * POOL : (j + 1) * POOL], axis=0, keepdims=True) for j in range(TOK // POOL)],
                axis=0,
            )
            * (1.0 / POOL)
        )
    land = jnp.concatenate(parts, axis=1)
    land_ref[...] = jnp.broadcast_to(land.astype(BF16)[None], land_ref.shape)


def pool(key_rows, value_rows):
    return pl.pallas_call(
        pool_kernel,
        out_shape=(
            jax.ShapeDtypeStruct((TOK, 512), BF16),
            jax.ShapeDtypeStruct((len(FIRST[0]), TOK // POOL, 512), BF16),
        ),
        compiler_params=pltpu.CompilerParams(vmem_limit_bytes=4 * 2**20),
    )(key_rows, value_rows)


def land_block(row):
    first = (row >> 2) & 63
    y, x, z = first >> 3, row >> 8, first & 7
    return y * 32 + x * 8 + z


def token_pick(rows):
    token = lax.broadcasted_iota(jnp.int32, (rows, HD), 0) & (TOK - 1)
    return jnp.where(token == lax.broadcasted_iota(jnp.int32, (rows, HD), 1), 1.0, 0.0).astype(BF16)


def land_bias(shape, axis):
    row = lax.broadcasted_iota(jnp.int32, shape, axis)
    return jnp.where(land_block(row) < lax.axis_index("ctx"), 0.0, BIG).astype(BF16)


def two_heads(ref, low):
    both = ref[:, pl.ds(low, 2 * HD)]
    return jnp.concatenate([both[:, :HD], both[:, HD:]], axis=0)


def side_by_side(rows):
    return jnp.concatenate([rows[:TOK], rows[TOK:]], axis=1)


def add(total, term):
    return term if total is None else total + term


def fold(combine, total, wide):
    for low in range(0, wide.shape[1], 128):
        piece = wide[:, low : low + 128]
        total = piece if total is None else combine(total, piece)
    return total


def cut(low, high):
    return [slice(at, at + CHUNK) for at in range(low, high, CHUNK)]


def attend_kernel(
    ctx_count,
    keep_ref,
    q_ref,
    do_ref,
    own_ref,
    p0_ref,
    p1_ref,
    p2_ref,
    land_ref,
    att_ref,
    dq_ref,
    stats_ref,
    own_grad_ref,
    g0_ref,
    g1_ref,
    g2_ref,
    keys,
    keys_t,
    values,
    values_t,
    work,
    dk,
    dv,
):
    block = lax.axis_index("ctx")
    n_keys = values.shape[0]
    n_local = TOK * (1 + LEVELS)

    row = lax.broadcasted_iota(jnp.int32, (TOK, TOK), 0)
    col = lax.broadcasted_iota(jnp.int32, (TOK, TOK), 1)
    keys_t[HD:, :TOK] = jnp.where(col > row, BIG, 0.0).astype(BF16)
    for level in range(LEVELS):
        distance = ctx_count // 2 ** (level + 1)
        wanted = jnp.logical_and((block // distance) % 2 == 1, keep_ref[0, level] == 1)
        bias = jnp.where(wanted, 0.0, BIG)
        keys_t[HD:, TOK * (level + 1) : TOK * (level + 2)] = jnp.full((HD, TOK), bias, F32).astype(BF16)
    keys_t[HD:, n_local:] = land_bias((HD, n_keys - n_local), 1)
    stats_ref[...] = jnp.zeros_like(stats_ref)
    pick = token_pick(2 * TOK)
    lane = lax.broadcasted_iota(jnp.int32, (2 * TOK, 128), 1)

    for head in range(2):
        k_cols = slice(head * HD, (head + 1) * HD)
        v_cols = slice(256 + head * HD, 256 + (head + 1) * HD)
        for number, ref in enumerate((own_ref, p0_ref, p1_ref, p2_ref)):
            rows = slice(number * TOK, (number + 1) * TOK)
            k_rows = ref[:, k_cols]
            v_rows = ref[:, v_cols]
            keys[rows, :] = k_rows
            keys_t[:HD, rows] = k_rows.T
            values[rows, :] = v_rows
            values_t[:, rows] = v_rows.T
        keys_t[:HD, n_local:] = land_ref[:, k_cols].T
        values[n_local:, :] = land_ref[:, v_cols]
        dk[...] = jnp.zeros_like(dk)
        dv[...] = jnp.zeros_like(dv)

        @pl.loop(0, 4)
        def _(step):
            number = head * 4 + step
            low = pl.multiple_of(number * 2 * HD, 2 * HD)
            q = two_heads(q_ref, low)
            do = two_heads(do_ref, low)
            q_pick = jnp.concatenate([q, pick], axis=1)

            peak = None
            for chunk in cut(0, n_keys):
                score = mul(q_pick, keys_t[:, chunk], NN) * (SCALE * LOG2E)
                work[:, chunk] = score
                peak = fold(jnp.maximum, peak, score)
            peak = jnp.max(peak, axis=1, keepdims=True)
            total = out = None
            for chunk in cut(0, n_keys):
                prob = jnp.exp2(work[:, chunk] - peak)
                if chunk.start < n_local:
                    work[:, chunk] = prob
                total = fold(jnp.add, total, prob)
                out = add(out, mul(prob.astype(BF16), values[chunk, :], NN))
            total = jnp.sum(total, axis=1, keepdims=True)
            inverse = 1.0 / total
            out = (out * inverse).astype(BF16)
            att_ref[:, pl.ds(low, 2 * HD)] = side_by_side(out)
            delta = jnp.sum(do.astype(F32) * out.astype(F32), axis=1, keepdims=True)
            stats = jnp.where(lane == 2 * number, peak + jnp.log2(total), stats_ref[...])
            stats_ref[...] = jnp.where(lane == 2 * number + 1, delta, stats)
            dq = None
            for chunk in cut(0, n_local):
                soft = work[:, chunk] * inverse
                dv[chunk, :] += mul(soft.astype(BF16), do, TN)
                dsoft = mul(do, values_t[:, chunk], NN)
                dscore = (soft * (dsoft - delta)).astype(BF16)
                dq = add(dq, mul(dscore, keys[chunk, :], NN))
                dk[chunk, :] += mul(dscore, q, TN)
            dq_ref[:, pl.ds(low, 2 * HD)] = side_by_side(dq)

        for source, factor, low in ((dk, SCALE, head * HD), (dv, 1.0, 256 + head * HD)):
            own_grad_ref[:, low : low + HD] = source[:TOK, :] * factor
            for level, ref in enumerate((g0_ref, g1_ref, g2_ref)):
                part = source[TOK * (level + 1) : TOK * (level + 2), :] * factor
                ref[:, low : low + HD] = part.astype(BF16)


def attend(ctx_count, partner_keep, queries, out_grad, own, partners, land):
    n_local = TOK * (1 + LEVELS)
    n_keys = n_local + land.shape[0]
    vmem = pl.BlockSpec(memory_space=pltpu.VMEM)
    return pl.pallas_call(
        functools.partial(attend_kernel, ctx_count),
        in_specs=[pl.BlockSpec(memory_space=pltpu.SMEM)] + [vmem] * 7,
        out_specs=[vmem] * 7,
        out_shape=[
            jax.ShapeDtypeStruct((TOK, 2048), BF16),
            jax.ShapeDtypeStruct((TOK, 2048), F32),
            jax.ShapeDtypeStruct((2 * TOK, 128), F32),
            jax.ShapeDtypeStruct((TOK, 512), F32),
        ]
        + [jax.ShapeDtypeStruct((TOK, 512), BF16)] * LEVELS,
        scratch_shapes=[
            pltpu.VMEM((n_local, HD), BF16),
            pltpu.VMEM((2 * HD, n_keys), BF16),
            pltpu.VMEM((n_keys, HD), BF16),
            pltpu.VMEM((HD, n_local), BF16),
            pltpu.VMEM((2 * TOK, n_keys), F32),
            pltpu.VMEM((n_local, HD), F32),
            pltpu.VMEM((n_local, HD), F32),
        ],
        compiler_params=pltpu.CompilerParams(vmem_limit_bytes=24 * 2**20),
        cost_estimate=pl.CostEstimate(flops=5 * 10**9, bytes_accessed=4 * 2**20, transcendentals=4 * 10**6),
    )(partner_keep, queries, out_grad, own, *partners, land)


def land_kernel(q_ref, do_ref, land_ref, part_ref, stats_ref, dq_ref, keys, keys_t, values_t):
    n_keys = keys.shape[0]
    keys_t[HD:, :] = land_bias((HD, n_keys), 1)
    pick = token_pick(2 * TOK)
    lane = lax.broadcasted_iota(jnp.int32, (2 * TOK, 128), 1)
    for head in range(2):
        keys[...] = land_ref[:, head * HD : (head + 1) * HD]
        keys_t[:HD, :] = keys[...].T
        values_t[...] = land_ref[:, 256 + head * HD : 256 + (head + 1) * HD].T

        @pl.loop(0, 4)
        def _(step):
            number = head * 4 + step
            low = pl.multiple_of(number * 2 * HD, 2 * HD)
            q = two_heads(q_ref, low)
            do = two_heads(do_ref, low)
            q_pick = jnp.concatenate([q, pick], axis=1)
            stats = stats_ref[...]
            log_sum = jnp.sum(jnp.where(lane == 2 * number, stats, 0.0), axis=1, keepdims=True)
            delta = jnp.sum(jnp.where(lane == 2 * number + 1, stats, 0.0), axis=1, keepdims=True)
            dq = two_heads(part_ref, low)
            for chunk in cut(0, n_keys):
                score = mul(q_pick, keys_t[:, chunk], NN) * (SCALE * LOG2E)
                soft = jnp.exp2(score - log_sum)
                dsoft = mul(do, values_t[:, chunk], NN)
                dscore = (soft * (dsoft - delta)).astype(BF16)
                dq = dq + mul(dscore, keys[chunk, :], NN)
            dq_ref[:, pl.ds(low, 2 * HD)] = side_by_side((SCALE * dq).astype(BF16))


def land_backward(queries, out_grad, land, part, stats):
    vmem = pl.BlockSpec(memory_space=pltpu.VMEM)
    n_keys = land.shape[0]
    return pl.pallas_call(
        land_kernel,
        in_specs=[vmem] * 5,
        out_specs=vmem,
        out_shape=jax.ShapeDtypeStruct((TOK, 2048), BF16),
        scratch_shapes=[
            pltpu.VMEM((n_keys, HD), BF16),
            pltpu.VMEM((2 * HD, n_keys), BF16),
            pltpu.VMEM((HD, n_keys), BF16),
        ],
        compiler_params=pltpu.CompilerParams(vmem_limit_bytes=24 * 2**20),
        cost_estimate=pl.CostEstimate(flops=4 * 10**9, bytes_accessed=4 * 2**20, transcendentals=2 * 10**6),
    )(queries, out_grad, land, part, stats)


def total_kernel(own_ref, r0_ref, r1_ref, r2_ref, sum_ref):
    total = own_ref[...]
    for ref in (r0_ref, r1_ref, r2_ref):
        total = total + ref[...].astype(F32)
    sum_ref[...] = total.astype(BF16)


def exchange(rows, groups):
    return lax.all_to_all(rows, "ctx", 0, 0, axis_index_groups=groups, tiled=True)


def local(queries, key_rows, value_rows, out_grad, partner_keep):
    ctx_count = lax.axis_size("ctx")
    own, land = pool(key_rows, value_rows)
    pairs = []
    for level in range(LEVELS):
        distance = ctx_count // 2 ** (level + 1)
        pairs.append([(b, b + distance) for b in range(ctx_count) if b // distance % 2 == 0])
    partners = [lax.ppermute(own, "ctx", pair) for pair in pairs]
    land = exchange(land, FIRST)
    land, partners = lax.optimization_barrier((land, partners))
    land = jnp.broadcast_to(land.reshape(1, -1, 512), (len(SECOND[0]), land.shape[0] * land.shape[1], 512))
    land = exchange(land, SECOND).reshape(-1, 512)
    att, part, stats, own_grad, *sent = attend(ctx_count, partner_keep, queries, out_grad, own, partners, land)
    dq = land_backward(queries, out_grad, land, part, stats)
    back = [
        lax.ppermute(part, "ctx", [(later, earlier) for earlier, later in pair]) for part, pair in zip(sent, pairs)
    ]
    total = pl.pallas_call(
        total_kernel,
        out_shape=jax.ShapeDtypeStruct((TOK, 512), BF16),
        compiler_params=pltpu.CompilerParams(vmem_limit_bytes=4 * 2**20),
    )(own_grad, *back)
    both = lax.all_gather(total, "head", axis=0)
    key_grad = jnp.concatenate([both[0, :, :256], both[1, :, :256]], axis=1)
    value_grad = jnp.concatenate([both[0, :, 256:], both[1, :, 256:]], axis=1)
    return att, dq, key_grad, value_grad


def solution(mesh):
    placed = (P("ctx", "head"), P("ctx", None), P("ctx", None), P("ctx", "head"), P("ctx", None))
    return jax.shard_map(
        local,
        mesh=mesh,
        in_specs=placed,
        out_specs=(P("ctx", "head"), P("ctx", "head"), P("ctx", None), P("ctx", None)),
        check_vma=False,
    )
```

time: 93.8 us -> 89.4 us (0.953); the launches traced: 92.1 us -> 89.1 us
  starting transfers between devices: 22.3 us -> 32.4 us
  blocking collectives: 28.1 us -> 21.1 us
  waiting for transfers between devices: 15.8 us -> 8.86 us
  Pallas kernels: 21.1 us -> 22.6 us
    all_to_all x1, starting transfers between devices: 6.5 us -> 15.6 us  [exchange(): lax.all_to_all(rows, 'ctx', 0, 0, axis_index_groups=groups, tiled=True)]
    all_to_all x1, blocking collectives: 23.2 us -> 16.7 us  [exchange(): lax.all_to_all(rows, 'ctx', 0, 0, axis_index_groups=groups, tiled=True)]
    pallas_call x1 -> x2, Pallas kernels: 17.6 us -> 21.8 us  [the longest x1 13.1 us: attend(): pl.pallas_call(functools.partial(attend_kernel, ctx_count), in_specs=[pl....]
    ppermute x3, waiting for transfers between devices: 12.6 us -> 8.85 us  [local(): partners = [lax.ppermute(own, 'ctx', pair) for pair in pairs]]
    ppermute x3, waiting for transfers between devices: 3.21 us -> 0.01 us  [local(): lax.ppermute(part, 'ctx', [(later, earlier) for earlier, later in pair])]
    pallas_call x1, Pallas kernels: 1.82 us -> 0.06 us  [local(): pl.pallas_call(total_kernel, out_shape=jax.ShapeDtypeStruct((TOK, 512), B...]
    unnamed x16 -> x10, local copies, waits for them, and re-layouts: 1.35 us -> 2.46 us
    ppermute x3, starting transfers between devices: 11.9 us -> 12.9 us  [local(): lax.ppermute(part, 'ctx', [(later, earlier) for earlier, later in pair])]
  transfers between devices with their start and end apart: 7 -> 7, of which waited for: 3 -> 2; matrix products, arithmetic and copies ran while one was open for 0% -> 0% of each run, Pallas kernels for 0% -> 10%
where the time goes in v2:
time: 89.4 us; the launch traced here: 89.1 us
  starting transfers between devices  32.4 us (36%)
  Pallas kernels  22.6 us (25%)
  blocking collectives  21.1 us (24%)
  waiting for transfers between devices  8.86 us (10%)
  local copies, waits for them, and re-layouts  2.62 us (3%)
    all_to_all x1, blocking collectives, exchange(): lax.all_to_all(rows, 'ctx', 0, 0, axis_index_groups=groups, tiled=True)  16.7 us
    all_to_all x1, starting transfers between devices, exchange(): lax.all_to_all(rows, 'ctx', 0, 0, axis_index_groups=groups, tiled=True)  15.6 us
    pallas_call x1, Pallas kernels, attend(): pl.pallas_call(functools.partial(attend_kernel, ctx_count), in_specs=[pl....  13.1 us
    ppermute x3, starting transfers between devices, local(): lax.ppermute(part, 'ctx', [(later, earlier) for earlier, later in pair])  12.9 us
    ppermute x3, waiting for transfers between devices, local(): partners = [lax.ppermute(own, 'ctx', pair) for pair in pairs]  8.85 us
    pallas_call x1, Pallas kernels, land_backward(): pl.pallas_call(land_kernel, in_specs=[vmem] * 5, out_specs=vmem, out_shap...  8.7 us
    all_gather x1, blocking collectives, local(): both = lax.all_gather(total, 'head', axis=0)  4.42 us
    ppermute x3, starting transfers between devices, local(): partners = [lax.ppermute(own, 'ctx', pair) for pair in pairs]  3.88 us
  transfers between devices with their start and end apart: 7, of which 2 were waited for; matrix products, arithmetic and copies ran while one was open for 0% of the time, Pallas kernels for 10%

profile of v2, /device:TPU:57, one launch (start us, length us, event | category | flops | bytes accessed | tf_op | source)
XLA Modules:
  0.0 89.1 jit_solution(4699828632755562904)
XLA Ops:
  0.6 0.0 copy-start
  0.6 0.9 %copy-done = bf16[128,512]{1,0:T(8,128)(2,1)S(1)} copy-done((bf16[128,512]{1,0:T(8,128)(2,1)S(1)}, bf16[128,512]{1,0:T(8,128)(2,1)}, u32[]{:S(2)}) %copy-start) | copy-done | bytes 131096
  1.5 0.0 copy-start.1
  1.5 0.9 %copy-done.1 = bf16[128,512]{1,0:T(8,128)(2,1)S(1)} copy-done((bf16[128,512]{1,0:T(8,128)(2,1)S(1)}, bf16[128,512]{1,0:T(8,128)(2,1)}, u32[]{:S(2)}) %copy-start.1) | copy-done | bytes 131096
  2.4 0.8 shard_map.84
  3.2 15.6 %all-to-all-start = ((bf16[64,4,512]{2,1,0:T(4,128)(2,1)}), bf16[64,4,512]{2,1,0:T(4,128)(2,1)S(1)}, u32[]{:S(2)}, u32[]{:S(2)}) async-start(bf16[64,4,512]{2,1,0:T(4,128)(2,1)} %get-tuple-element.18), calls=%async_computation | async-start | bytes 524288 | tf_op jit(solution)/shard_map/all_to_all | solution.py:289
  18.8 1.3 %collective-permute-start.2 = (bf16[128,512]{1,0:T(8,128)(2,1)S(1)}, bf16[128,512]{1,0:T(8,128)(2,1)S(1)}, u32[]{:S(2)}, u32[]{:S(2)}) collective-permute-start(bf16[128,512]{1,0:T(8,128)(2,1)S(1)} %get-tuple-element.17.own_ref), channel_id=1, source_target_pairs={{0,32},{1,33},{2,34},{3,35},{4,36},{5,37},{6,38},{7,39},{8,40},{9,... | collective-permute-start | bytes 393224 | tf_op jit(solution)/shard_map/ppermute | solution.py:299
  20.1 1.3 %collective-permute-start.1 = (bf16[128,512]{1,0:T(8,128)(2,1)S(1)}, bf16[128,512]{1,0:T(8,128)(2,1)S(1)}, u32[]{:S(2)}, u32[]{:S(2)}) collective-permute-start(bf16[128,512]{1,0:T(8,128)(2,1)S(1)} %get-tuple-element.17.own_ref), channel_id=1, source_target_pairs={{0,64},{1,65},{2,66},{3,67},{4,68},{5,69},{6,70},{7,71},{8,72},{9,... | collective-permute-start | bytes 393224 | tf_op jit(solution)/shard_map/ppermute | solution.py:299
  21.4 1.3 %collective-permute-start = (bf16[128,512]{1,0:T(8,128)(2,1)S(1)}, bf16[128,512]{1,0:T(8,128)(2,1)S(1)}, u32[]{:S(2)}, u32[]{:S(2)}) collective-permute-start(bf16[128,512]{1,0:T(8,128)(2,1)S(1)} %get-tuple-element.17.own_ref), channel_id=1, source_target_pairs={{0,128},{1,129},{2,130},{3,131},{4,132},{5,133},{6,134},{7,135},{8... | collective-permute-start | bytes 393224 | tf_op jit(solution)/shard_map/ppermute | solution.py:299
  22.7 8.4 %collective-permute-done.2.p2_ref = bf16[128,512]{1,0:T(8,128)(2,1)S(1)} collective-permute-done((bf16[128,512]{1,0:T(8,128)(2,1)S(1)}, bf16[128,512]{1,0:T(8,128)(2,1)S(1)}, u32[]{:S(2)}, u32[]{:S(2)}) %collective-permute-start.2) | collective-permute-done | bytes 131104 | tf_op jit(solution)/shard_map/ppermute | solution.py:299
  31.1 0.0 collective-permute-done.1.p1_ref
  31.1 0.5 collective-permute-done.p0_ref
  31.6 0.0 all-to-all-done
  31.6 0.1 broadcast_in_dim.7
  31.6 0.1 broadcast_in_dim.8
  31.7 0.0 copy-start.2
  31.7 0.0 copy-start.3
  31.7 16.7 %all_to_all.10 = bf16[4,256,512]{2,1,0:T(8,128)(2,1)S(1)} all-to-all(bf16[4,256,512]{2,1,0:T(8,128)(2,1)S(1)} %broadcast_in_dim.8), channel_id=1, replica_groups={{0,8,16,24},{1,9,17,25},{2,10,18,26},{3,11,19,27},{4,12,20,28},{5,13,21..., dimensions={0} | all-to-all | bytes 2097152 | tf_op jit(solution)/shard_map/all_to_all | solution.py:289
  48.4 0.0 copy-done.2
  48.4 0.0 copy-done.3
  48.4 0.6 copy-done.4
  49.1 13.1 %shard_map.85 = (bf16[128,2048]{1,0:T(8,128)(2,1)}, f32[128,2048]{1,0:T(8,128)S(1)}, f32[256,128]{1,0:T(8,128)S(1)}, f32[128,512]{1,0:T(8,128)S(1)}, bf16[128,51...) custom-call(s32[1,3]{1,0:T(1,128)S(1)} %copy-done.4, ...), custom_call_target="tpu_custom_call" | custom-call | flops 5000000000 | bytes 4194304 | tf_op jit(solution)/shard_map/pallas_call | solution.py:208
  62.2 2.8 %collective-permute-start.3 = (bf16[128,512]{1,0:T(8,128)(2,1)S(1)}, bf16[128,512]{1,0:T(8,128)(2,1)S(1)}, u32[]{:S(2)}, u32[]{:S(2)}) collective-permute-start(bf16[128,512]{1,0:T(8,128)(2,1)S(1)} %get-tuple-element.27), channel_id=1, source_target_pairs={{128,0},{129,1},{130,2},{131,3},{132,4},{133,5},{134,6},{135,7},{1... | collective-permute-start | bytes 393224 | tf_op jit(solution)/shard_map/ppermute | solution.py:307
  64.9 8.0 %collective-permute-start.4 = (bf16[128,512]{1,0:T(8,128)(2,1)S(1)}, bf16[128,512]{1,0:T(8,128)(2,1)S(1)}, u32[]{:S(2)}, u32[]{:S(2)}) collective-permute-start(bf16[128,512]{1,0:T(8,128)(2,1)S(1)} %get-tuple-element.28), channel_id=1, source_target_pairs={{64,0},{65,1},{66,2},{67,3},{68,4},{69,5},{70,6},{71,7},{72,8},{73... | collective-permute-start | bytes 393224 | tf_op jit(solution)/shard_map/ppermute | solution.py:307
  73.0 2.2 %collective-permute-start.5 = (bf16[128,512]{1,0:T(8,128)(2,1)S(1)}, bf16[128,512]{1,0:T(8,128)(2,1)S(1)}, u32[]{:S(2)}, u32[]{:S(2)}) collective-permute-start(bf16[128,512]{1,0:T(8,128)(2,1)S(1)} %get-tuple-element.29), channel_id=1, source_target_pairs={{32,0},{33,1},{34,2},{35,3},{36,4},{37,5},{38,6},{39,7},{40,8},{41... | collective-permute-start | bytes 393224 | tf_op jit(solution)/shard_map/ppermute | solution.py:307
  75.1 8.7 %shard_map.86 = bf16[128,2048]{1,0:T(8,128)(2,1)} custom-call(bf16[128,2048]{1,0:T(8,128)(2,1)S(1)} %copy-done.2, bf16[128,2048]{1,0:T(8,128)(2,1)S(1)} %copy-done.3, bf16[1024,512]{1,0:T(8,128)(2,1)S(1)} %bitcast.11, f32[128,2048]{1,0:T(8,128)S(1)} %get-tuple-element.24.part_ref, f32[256,128]{1,0:T(8,128)S(1)} %get-tuple-element.25.stats_ref), custom_call_target="tpu_custom_call" | custom-call | flops 4000000000 | bytes 4194304 | tf_op jit(solution)/shard_map/pallas_call | solution.py:266
  83.8 0.0 collective-permute-done.3.r0_ref
  83.8 0.0 collective-permute-done.4.r1_ref
  83.8 0.0 collective-permute-done.5.r2_ref
  83.8 0.1 shard_map.87
  83.9 4.4 %all-gather = bf16[256,512]{1,0:T(8,128)(2,1)S(1)} all-gather(bf16[128,512]{1,0:T(8,128)(2,1)S(1)} %shard_map.87), channel_id=2, replica_groups=mesh['head'=2,'ctx'=256] {'head'}, dimensions={0}, use_global_device_ids=true | all-gather | bytes 393216 | tf_op jit(solution)/shard_map/all_gather | solution.py:314
  88.3 0.7 pad_maximum_fusion
  (2 shorter events, 0.0 us)
Async XLA Ops:
  0.6 0.9 %copy-start = (bf16[128,512]{1,0:T(8,128)(2,1)S(1)}, bf16[128,512]{1,0:T(8,128)(2,1)}, u32[]{:S(2)}) copy-start(bf16[128,512]{1,0:T(8,128)(2,1)} %key_ref.1) | copy-start | bytes 393220
  1.5 0.9 %copy-start.1 = (bf16[128,512]{1,0:T(8,128)(2,1)S(1)}, bf16[128,512]{1,0:T(8,128)(2,1)}, u32[]{:S(2)}) copy-start(bf16[128,512]{1,0:T(8,128)(2,1)} %value_ref.1) | copy-start | bytes 393220
  3.2 28.4 %all-to-all-start = ((bf16[64,4,512]{2,1,0:T(4,128)(2,1)}), bf16[64,4,512]{2,1,0:T(4,128)(2,1)S(1)}, u32[]{:S(2)}, u32[]{:S(2)}) async-start(bf16[64,4,512]{2,1,0:T(4,128)(2,1)} %get-tuple-element.18), calls=%async_computation | async-start | bytes 524288 | tf_op jit(solution)/shard_map/all_to_all | solution.py:289
  18.8 12.3 %collective-permute-start.2 = (bf16[128,512]{1,0:T(8,128)(2,1)S(1)}, bf16[128,512]{1,0:T(8,128)(2,1)S(1)}, u32[]{:S(2)}, u32[]{:S(2)}) collective-permute-start(bf16[128,512]{1,0:T(8,128)(2,1)S(1)} %get-tuple-element.17.own_ref), channel_id=1, source_target_pairs={{0,32},{1,33},{2,34},{3,35},{4,36},{5,37},{6,38},{7,39},{8,40},{9,... | collective-permute-start | bytes 393224 | tf_op jit(solution)/shard_map/ppermute | solution.py:299
  20.1 11.0 %collective-permute-start.1 = (bf16[128,512]{1,0:T(8,128)(2,1)S(1)}, bf16[128,512]{1,0:T(8,128)(2,1)S(1)}, u32[]{:S(2)}, u32[]{:S(2)}) collective-permute-start(bf16[128,512]{1,0:T(8,128)(2,1)S(1)} %get-tuple-element.17.own_ref), channel_id=1, source_target_pairs={{0,64},{1,65},{2,66},{3,67},{4,68},{5,69},{6,70},{7,71},{8,72},{9,... | collective-permute-start | bytes 393224 | tf_op jit(solution)/shard_map/ppermute | solution.py:299
  21.4 10.2 %collective-permute-start = (bf16[128,512]{1,0:T(8,128)(2,1)S(1)}, bf16[128,512]{1,0:T(8,128)(2,1)S(1)}, u32[]{:S(2)}, u32[]{:S(2)}) collective-permute-start(bf16[128,512]{1,0:T(8,128)(2,1)S(1)} %get-tuple-element.17.own_ref), channel_id=1, source_target_pairs={{0,128},{1,129},{2,130},{3,131},{4,132},{5,133},{6,134},{7,135},{8... | collective-permute-start | bytes 393224 | tf_op jit(solution)/shard_map/ppermute | solution.py:299
  31.7 16.7 %copy-start.2 = (bf16[128,2048]{1,0:T(8,128)(2,1)S(1)}, bf16[128,2048]{1,0:T(8,128)(2,1)}, u32[]{:S(2)}) copy-start(bf16[128,2048]{1,0:T(8,128)(2,1)} %q_ref.3) | copy-start | bytes 1572868
  31.7 16.7 %copy-start.3 = (bf16[128,2048]{1,0:T(8,128)(2,1)S(1)}, bf16[128,2048]{1,0:T(8,128)(2,1)}, u32[]{:S(2)}) copy-start(bf16[128,2048]{1,0:T(8,128)(2,1)} %do_ref.3) | copy-start | bytes 1572868
  48.4 0.7 copy-start.4
  62.2 21.6 %collective-permute-start.3 = (bf16[128,512]{1,0:T(8,128)(2,1)S(1)}, bf16[128,512]{1,0:T(8,128)(2,1)S(1)}, u32[]{:S(2)}, u32[]{:S(2)}) collective-permute-start(bf16[128,512]{1,0:T(8,128)(2,1)S(1)} %get-tuple-element.27), channel_id=1, source_target_pairs={{128,0},{129,1},{130,2},{131,3},{132,4},{133,5},{134,6},{135,7},{1... | collective-permute-start | bytes 393224 | tf_op jit(solution)/shard_map/ppermute | solution.py:307
  64.9 18.9 %collective-permute-start.4 = (bf16[128,512]{1,0:T(8,128)(2,1)S(1)}, bf16[128,512]{1,0:T(8,128)(2,1)S(1)}, u32[]{:S(2)}, u32[]{:S(2)}) collective-permute-start(bf16[128,512]{1,0:T(8,128)(2,1)S(1)} %get-tuple-element.28), channel_id=1, source_target_pairs={{64,0},{65,1},{66,2},{67,3},{68,4},{69,5},{70,6},{71,7},{72,8},{73... | collective-permute-start | bytes 393224 | tf_op jit(solution)/shard_map/ppermute | solution.py:307
  73.0 10.9 %collective-permute-start.5 = (bf16[128,512]{1,0:T(8,128)(2,1)S(1)}, bf16[128,512]{1,0:T(8,128)(2,1)S(1)}, u32[]{:S(2)}, u32[]{:S(2)}) collective-permute-start(bf16[128,512]{1,0:T(8,128)(2,1)S(1)} %get-tuple-element.29), channel_id=1, source_target_pairs={{32,0},{33,1},{34,2},{35,3},{36,4},{37,5},{38,6},{39,7},{40,8},{41... | collective-permute-start | bytes 393224 | tf_op jit(solution)/shard_map/ppermute | solution.py:307
